TPU v7x, 32 devices: a whole 2x2x4 slice. The times are simulated.
32 devices in a mesh: groups: 2 (over y), vocab: 4 (over z), dp: 2 (over x), rep: 2 (over core).
Axes of the slice: x: 2, y: 2, z: 4, core: 2. Of those that a mesh axis runs over, the one named last changes fastest.
Arguments:
- hidden: bfloat16 [512, 4608], P(('groups', 'dp', 'rep')), parts along dimension 0, may hold values from -6 to 6
- cotangent: bfloat16 [512, 4608], P(('groups', 'dp', 'rep')), parts along dimension 0, may hold values from -0.09375 to 0.09375
- table: bfloat16 [1024, 4608], P('vocab', ('dp', 'rep')), may hold values from -0.25 to 0.25
- token_ids: int32 [512], P('groups'), parts along dimension 0, may hold values from 0 to 1023
- target_ids: int32 [512], P('groups'), parts along dimension 0, may hold values from 0 to 1023
- row_counts: int32 [8], P('groups'), parts along dimension 0, may hold values from 16 to 64
Outputs:
- hidden_grad: bfloat16 [512, 4608], P('groups', ('dp', 'rep')), parts along dimension 0
- table_grad: bfloat16 [2048, 4608], P(('groups', 'vocab'), ('dp', 'rep')), parts along dimension 0
There are 2 independent parts, one for each index of `groups`. A program takes and returns all parts, laid end to end along the dimension named above; an argument that names none is the same for every part. Nothing has to cross between parts.
All inputs are finite; a program needn't handle non-finite values.
Results may differ from a plain program's by a relative error of at most 0.0049.
Values may be sent and summed in bfloat16 or wider, within the bound.
A program may use at most 64 MiB of HBM per device.

v0:
```python
import math

import jax
import jax.numpy as jnp
from jax import lax
from jax.sharding import PartitionSpec as P

D = 4608
CAP = 30
ROW_LEN = 64


def token_weights(row_counts):
    slots = jnp.arange(ROW_LEN, dtype=jnp.int32)[None, :]
    counts = row_counts[:, None]
    scale = ROW_LEN / counts.astype(jnp.float32)
    return jnp.where(slots < counts, scale, jnp.float32(0.0)).reshape(-1)


def shards(hidden, cotangent, table, token_ids, target_ids, row_counts):
    h_cols, g_cols = (
        lax.all_to_all(hidden, ("dp", "rep"), split_axis=1, concat_axis=0, tiled=True),
        lax.all_to_all(cotangent, ("dp", "rep"), split_axis=1, concat_axis=0, tiled=True),
    )
    block = table.shape[0]
    parts = lax.axis_size(("dp", "rep"))
    base = lax.axis_index("vocab") * block
    weight = token_weights(row_counts)
    span = block // parts
    raw = lax.psum_scatter(
        lax.dot_general(
            table, h_cols, (((1,), (1,)), ((), ())), preferred_element_type=jnp.float32
        ),
        ("dp", "rep"),
        scatter_dimension=0,
        tiled=True,
    )
    first = base + lax.axis_index(("dp", "rep")) * span
    squash = jnp.tanh(raw / CAP)
    expo = jnp.exp(CAP * squash)
    total = lax.psum(jnp.sum(expo, axis=0), ("vocab", "dp", "rep"))
    row_ids = first + jnp.arange(span, dtype=jnp.int32)
    hit = (target_ids[None, :] == row_ids[:, None]).astype(jnp.float32)
    grad = (weight[None, :] * (expo / total[None, :] - hit) * (1.0 - squash * squash)).astype(
        jnp.bfloat16
    )
    grads = lax.all_gather(grad, ("dp", "rep"), axis=0, tiled=True)
    head = jnp.dot(grads, h_cols, preferred_element_type=jnp.float32)
    partial_sum = lax.dot_general(
        grads, table, (((0,), (0,)), ((), ())), preferred_element_type=jnp.float32
    )
    block_ids = base + jnp.arange(block, dtype=jnp.int32)
    one_hot = (token_ids[:, None] == block_ids[None, :]).astype(jnp.bfloat16)
    embed = lax.dot_general(
        one_hot, g_cols, (((0,), (0,)), ((), ())), preferred_element_type=jnp.float32
    )
    table_grad = (head + math.sqrt(D) * embed).astype(jnp.bfloat16)
    hidden_grad = lax.psum(partial_sum, "vocab").astype(jnp.bfloat16)
    return (hidden_grad, table_grad)


def solution(mesh):
    in_specs = (
        P(("groups", "dp", "rep"), None),
        P(("groups", "dp", "rep"), None),
        P("vocab", ("dp", "rep")),
        P("groups"),
        P("groups"),
        P("groups"),
    )
    out_specs = (P("groups", ("dp", "rep")), P(("groups", "vocab"), ("dp", "rep")))
    return jax.shard_map(shards, mesh=mesh, in_specs=in_specs, out_specs=out_specs, check_vma=False)
```

profile of v0, /device:TPU:0, one launch (start us, length us, event | category | flops | bytes accessed | tf_op | source)
XLA Modules:
  0.0 147.9 jit_solution(5367822230627518761)
XLA Ops:
  7.2 0.0 copy-start
  7.2 0.0 copy-start.1
  7.2 2.0 %copy.17 = bf16[8,4,8,1152]{3,2,0,1:T(8,128)(2,1)} copy(bf16[8,4,8,1152]{3,2,1,0:T(8,128)(2,1)} %bitcast.24) | data formatting | bytes 1179648 | tf_op jit(solution)/shard_map/all_to_all | solution.py:22
  9.2 0.0 copy-start.4
  9.2 4.3 %all-to-all-start = ((bf16[64,4,1152]{2,0,1:T(8,128)(2,1)}), bf16[64,4,1152]{2,0,1:T(8,128)(2,1)S(1)}, u32[]{:S(2)}, u32[]{:S(2)}) async-start(bf16[64,4,1152]{2,0,1:T(8,128)(2,1)} %bitcast.20), calls=%async_computation | async-start | bytes 1179648 | tf_op jit(solution)/shard_map/all_to_all | solution.py:22
  13.6 0.0 copy-done.1
  13.6 0.9 copy.16
  14.4 0.0 copy-done.4
  14.4 8.7 %all-to-all-done = bf16[64,4,1152]{2,0,1:T(8,128)(2,1)S(1)} async-done(((bf16[64,4,1152]{2,0,1:T(8,128)(2,1)}), bf16[64,4,1152]{2,0,1:T(8,128)(2,1)S(1)}, u32[]{:S(2)}, u32[]{:S(2)}) %all-to-all-start) | async-done | bytes 589856 | tf_op jit(solution)/shard_map/all_to_all | solution.py:22
  23.1 0.0 copy-start.2
  23.1 3.6 %all-to-all-start.1 = ((bf16[64,4,1152]{2,0,1:T(8,128)(2,1)}), bf16[64,4,1152]{2,0,1:T(8,128)(2,1)S(1)}, u32[]{:S(2)}, u32[]{:S(2)}) async-start(bf16[64,4,1152]{2,0,1:T(8,128)(2,1)} %bitcast.19), calls=%async_computation.2 | async-start | bytes 1179648 | tf_op jit(solution)/shard_map/all_to_all | solution.py:23
  26.7 0.0 reduce-scatter.2.cloned.1.call-start
  26.8 0.0 copy-done
  26.8 1.1 fusion.6
  27.9 0.0 copy-start.3
  27.9 0.0 reduce-scatter.2.cloned.1.call-update
  27.9 0.1 fusion.5
  28.0 0.1 select_n.12
  28.0 8.2 %all-to-all-done.1 = bf16[64,4,1152]{2,0,1:T(8,128)(2,1)S(1)} async-done(((bf16[64,4,1152]{2,0,1:T(8,128)(2,1)}), bf16[64,4,1152]{2,0,1:T(8,128)(2,1)S(1)}, u32[]{:S(2)}, u32[]{:S(2)}) %all-to-all-start.1) | async-done | bytes 589856 | tf_op jit(solution)/shard_map/all_to_all | solution.py:23
  36.2 0.0 copy-done.2
  36.2 0.5 convolution_multiply_fusion
  36.7 16.4 %reduce-scatter.2.cloned.1.call-done = f32[64,256]{1,0:T(8,128)} async-done(((f32[256,256]{1,0:T(8,128)}), f32[64,256]{1,0:T(8,128)}) %reduce-scatter.2.cloned.1.call-update) | async-done | bytes 65552 | tf_op jit(solution)/shard_map/reduce_scatter | solution.py:30
  53.1 0.9 fusion.4
  54.0 32.2 %psum.14 = f32[256]{0:T(256)S(1)} all-reduce(f32[256]{0:T(256)S(1)} %fusion.4), channel_id=1, replica_groups=mesh['groups'=2,'vocab'=4,'dp'=2,'rep'=2] {'vocab','dp','rep'}, use_global_device_ids=true, to_apply=%region_2.3 | all-reduce | flops 256 | bytes 2048 | tf_op jit(solution)/shard_map/psum | solution.py:41
  86.1 0.0 copy-done.3
  86.1 0.9 multiply_convert_fusion
  87.1 5.4 %all_gather.3 = bf16[256,256]{1,0:T(8,128)(2,1)S(1)} all-gather(bf16[64,256]{1,0:T(8,128)(2,1)S(1)} %multiply_convert_fusion), channel_id=1, replica_groups=mesh['groups'=2,'vocab'=4,'dp'=2,'rep'=2] {'dp','rep'}, dimensions={0}, use_global_device_ids=true | all-gather | bytes 163840 | tf_op jit(solution)/shard_map/all_gather | solution.py:47
  92.5 0.4 fusion.7
  92.9 1.2 fusion
  94.0 47.0 %all-reduce.1 = bf16[256,1152]{1,0:T(8,128)(2,1)} all-reduce(f32[256,1152]{1,0:T(8,128)S(1)} %fusion.7), channel_id=1, replica_groups=mesh['groups'=2,'vocab'=4,'dp'=2,'rep'=2] {'vocab'}, use_global_device_ids=true, to_apply=%region_3.4 | all-reduce | flops 294912 | bytes 1769472 | tf_op jit(solution)/shard_map/psum | solution.py:58
  (3 shorter events, 0.0 us)
Async XLA Ops:
  7.2 19.6 %copy-start = (bf16[256,1152]{1,0:T(8,128)(2,1)S(1)}, bf16[256,1152]{1,0:T(8,128)(2,1)}, u32[]{:S(2)}) copy-start(bf16[256,1152]{1,0:T(8,128)(2,1)} %param.8) | copy-start | bytes 1769476
  7.2 6.4 %copy-start.1 = (bf16[64,4608]{1,0:T(8,128)(2,1)S(1)}, bf16[64,4608]{1,0:T(8,128)(2,1)}, u32[]{:S(2)}) copy-start(bf16[64,4608]{1,0:T(8,128)(2,1)} %param.7) | copy-start | bytes 1769476
  9.2 5.2 %copy-start.4 = (s32[4]{0:T(128)S(1)}, s32[4]{0:T(128)}, u32[]{:S(2)}) copy-start(s32[4]{0:T(128)} %param.11) | copy-start | bytes 52
  9.2 13.9 %all-to-all-start = ((bf16[64,4,1152]{2,0,1:T(8,128)(2,1)}), bf16[64,4,1152]{2,0,1:T(8,128)(2,1)S(1)}, u32[]{:S(2)}, u32[]{:S(2)}) async-start(bf16[64,4,1152]{2,0,1:T(8,128)(2,1)} %bitcast.20), calls=%async_computation | async-start | bytes 1179648 | tf_op jit(solution)/shard_map/all_to_all | solution.py:22
  23.1 13.1 %copy-start.2 = (s32[256]{0:T(256)S(1)}, s32[256]{0:T(256)}, u32[]{:S(2)}) copy-start(s32[256]{0:T(256)} %param.9) | copy-start | bytes 3076
  23.1 13.1 %all-to-all-start.1 = ((bf16[64,4,1152]{2,0,1:T(8,128)(2,1)}), bf16[64,4,1152]{2,0,1:T(8,128)(2,1)S(1)}, u32[]{:S(2)}, u32[]{:S(2)}) async-start(bf16[64,4,1152]{2,0,1:T(8,128)(2,1)} %bitcast.19), calls=%async_computation.2 | async-start | bytes 1179648 | tf_op jit(solution)/shard_map/all_to_all | solution.py:23
  26.7 26.3 %reduce-scatter.2.cloned.1.call-start = ((), (), s32[]{:S(2)}) async-start(), calls=%async_computation.3 | async-start | bytes 327680 | tf_op jit(solution)/shard_map/reduce_scatter | solution.py:30
  27.9 58.3 %copy-start.3 = (s32[256]{0:T(256)S(1)}, s32[256]{0:T(256)}, u32[]{:S(2)}) copy-start(s32[256]{0:T(256)} %param.10) | copy-start | bytes 3076
Sparse Core Ops, SparseCore 0:
  30.6 22.4 reduce-scatter.1
where the time goes:
time: 148 us
  blocking collectives  84.6 us (57%)
  waiting for transfers between devices  33.2 us (22%)
  between operations  14.1 us (10%)
  starting transfers between devices  7.99 us (5%)
  matrix products  3.06 us (2%)
  local copies, waits for them, and re-layouts  2.99 us (2%)
  other arithmetic  1.89 us (1%)
    psum x1, blocking collectives, shards(): hidden_grad = lax.psum(partial_sum, 'vocab').astype(jnp.bfloat16)  47 us
    psum x1, blocking collectives, shards(): total = lax.psum(jnp.sum(expo, axis=0), ('vocab', 'dp', 'rep'))  32.2 us
    reduce_scatter x1, waiting for transfers between devices, shards(): lax.psum_scatter(lax.dot_general(table, h_cols, (((1,), (1,)), ((), ())),...  16.4 us
    all_to_all x1, waiting for transfers between devices, shards(): lax.all_to_all(hidden, ('dp', 'rep'), split_axis=1, concat_axis=0, tiled=...  8.67 us
    all_to_all x1, waiting for transfers between devices, shards(): lax.all_to_all(cotangent, ('dp', 'rep'), split_axis=1, concat_axis=0, til...  8.19 us
    all_gather x1, blocking collectives, shards(): grads = lax.all_gather(grad, ('dp', 'rep'), axis=0, tiled=True)  5.43 us
    all_to_all x1, starting transfers between devices, shards(): lax.all_to_all(hidden, ('dp', 'rep'), split_axis=1, concat_axis=0, tiled=...  4.34 us
    all_to_all x1, starting transfers between devices, shards(): lax.all_to_all(cotangent, ('dp', 'rep'), split_axis=1, concat_axis=0, til...  3.61 us
  transfers between devices with their start and end apart: 3, of which 3 were waited for; matrix products, arithmetic and copies ran while one was open for 2% of the time, Pallas kernels for 0%

commit v1 on v0

--- a/solution.py
+++ b/solution.py
@@ -3,6 +3,8 @@
 import jax
 import jax.numpy as jnp
 from jax import lax
+from jax.experimental import pallas as pl
+from jax.experimental.pallas import tpu as pltpu
 from jax.sharding import PartitionSpec as P
 
 D = 4608
@@ -17,7 +19,7 @@
     return jnp.where(slots < counts, scale, jnp.float32(0.0)).reshape(-1)
 
 
-def shards(hidden, cotangent, table, token_ids, target_ids, row_counts):
+def plain(hidden, cotangent, table, token_ids, target_ids, row_counts):
     h_cols, g_cols = (
         lax.all_to_all(hidden, ("dp", "rep"), split_axis=1, concat_axis=0, tiled=True),
         lax.all_to_all(cotangent, ("dp", "rep"), split_axis=1, concat_axis=0, tiled=True),
@@ -59,7 +61,226 @@
     return (hidden_grad, table_grad)
 
 
+MESH = pl.DeviceIdType.MESH
+TILE = 384
+
+
+def kernel(
+    hid, cot, tab, tok, tgt, cnt,
+    hid_out, tab_out,
+    tall, hcols, gcols, part, rawin, tot, gall, tcol,
+    loc_sem, h_snd, h_rcv, c_snd, c_rcv, tz_snd, tz_rcv, ty_snd, ty_rcv,
+    p_snd, p_rcv, s_snd, s_rcv, g_snd, g_rcv, f_snd, f_rcv,
+):
+    y, z = lax.axis_index("groups"), lax.axis_index("vocab")
+    x, c = lax.axis_index("dp"), lax.axis_index("rep")
+    p = 2 * x + c
+    cols = tab.shape[1]
+    block = tab.shape[0]
+    half = block // 2
+    near = {1: (x, 1 - c), 2: (1 - x, c), 3: (1 - x, 1 - c)}
+    near_id = {k: {"dp": a, "rep": b} for k, (a, b) in near.items()}
+    place = {0: p, **{k: 2 * a + b for k, (a, b) in near.items()}}
+    up_id = {d: {"vocab": lax.rem(z + d, 4)} for d in (1, 2, 3)}
+    down = {d: lax.rem(z + 4 - d, 4) for d in (1, 2, 3)}
+    twin = {"groups": 1 - y}
+
+    def remote(src, dst, snd, rcv, to):
+        return pltpu.make_async_remote_copy(
+            src_ref=src, dst_ref=dst, send_sem=snd, recv_sem=rcv, device_id=to, device_id_type=MESH
+        )
+
+    def my_cols(q):
+        return pl.ds(pl.multiple_of(q * cols, 128), cols)
+
+    own = [
+        pltpu.make_async_copy(hid.at[:, my_cols(p)], hcols.at[p], loc_sem.at[0]),
+        pltpu.make_async_copy(tab, tall.at[z], loc_sem.at[1]),
+        pltpu.make_async_copy(cot.at[:, my_cols(p)], gcols.at[p], loc_sem.at[2]),
+    ]
+    for copy in own:
+        copy.start()
+
+    barrier = pltpu.get_barrier_semaphore()
+    for to in (*near_id.values(), *up_id.values(), twin):
+        pl.semaphore_signal(barrier, inc=1, device_id=to, device_id_type=MESH)
+    pl.semaphore_wait(barrier, 7)
+
+    send_h = {
+        k: remote(hid.at[:, my_cols(place[k])], hcols.at[p], h_snd.at[k], h_rcv.at[k], near_id[k])
+        for k in (2, 3, 1)
+    }
+    for copy in send_h.values():
+        copy.start()
+    mine = pl.ds(pl.multiple_of(half * y, half), half)
+    send_t = {
+        d: remote(tab.at[mine], tall.at[z, mine], tz_snd.at[d], tz_rcv.at[d], up_id[d])
+        for d in (1, 3, 2)
+    }
+    for copy in send_t.values():
+        copy.start()
+
+    ids = jnp.broadcast_to(tgt[...].astype(jnp.float32), (128, tgt.shape[1]))
+    tcol[...] = ids.T
+
+    for copy in own:
+        copy.wait()
+    send_p = {}
+    for k in (0, 1, 2, 3):
+        if k:
+            send_h[k].wait_recv()
+        part[k] = lax.dot_general(
+            hcols[place[k]], tall[z], (((1,), (1,)), ((), ())), preferred_element_type=jnp.float32
+        )
+        if k:
+            send_p[k] = remote(part.at[k], rawin.at[k], p_snd.at[k], p_rcv.at[k], near_id[k])
+            send_p[k].start()
+    send_c = {
+        k: remote(cot.at[:, my_cols(place[k])], gcols.at[p], c_snd.at[k], c_rcv.at[k], near_id[k])
+        for k in (2, 3, 1)
+    }
+    for copy in send_c.values():
+        copy.start()
+
+    raw = part[0]
+    for k in (1, 2, 3):
+        send_p[k].wait_recv()
+        raw = raw + rawin[k]
+    squash = jnp.tanh(raw / CAP)
+    expo = jnp.exp(CAP * squash)
+    line = jnp.broadcast_to(jnp.sum(expo, axis=1, keepdims=True), (ROW_LEN, 128))
+    tot[0] = jnp.concatenate([line, line], axis=0).T[:8]
+    send_s = {d: remote(tot.at[0], tot.at[d], s_snd.at[d], s_rcv.at[d], up_id[d]) for d in (1, 2, 3)}
+    for copy in send_s.values():
+        copy.start()
+    target = tcol[pl.ds(pl.multiple_of(ROW_LEN * p, ROW_LEN), ROW_LEN), :]
+    target = jnp.concatenate([target] * (block // 128), axis=1)
+    row_ids = (z * block + lax.broadcasted_iota(jnp.int32, (ROW_LEN, block), 1)).astype(jnp.float32)
+    hit = (target == row_ids).astype(jnp.float32)
+    count = jnp.full((ROW_LEN, block), cnt[p], jnp.int32)
+    slot = lax.broadcasted_iota(jnp.int32, (ROW_LEN, block), 0)
+    weight = jnp.where(slot < count, ROW_LEN / count.astype(jnp.float32), 0.0)
+    slope = 1.0 - squash * squash
+    for copy in send_s.values():
+        copy.wait_recv()
+    whole = tot[0] + tot[1] + tot[2] + tot[3]
+    whole = jnp.broadcast_to(whole[:1], (128, 128)).T[:ROW_LEN]
+    whole = jnp.concatenate([whole] * (block // 128), axis=1)
+    gall[z, p] = (weight * (expo / whole - hit) * slope).astype(jnp.bfloat16)
+
+    send_g = {d: remote(gall.at[z, p], gall.at[z, p], g_snd.at[d], g_rcv.at[d], up_id[d]) for d in (1, 2, 3)}
+    for copy in send_g.values():
+        copy.start()
+    send_f = {}
+
+    def hand_on(d, row):
+        for k in (2, 3, 1):
+            piece = gall.at[row, p]
+            send_f[d, k] = remote(piece, piece, f_snd.at[d, k], f_rcv.at[d, k], near_id[k])
+            send_f[d, k].start()
+
+    hand_on(0, z)
+    send_y = {}
+    for d in (1, 3, 2):
+        send_g[d].wait_recv()
+        hand_on(d, down[d])
+        send_t[d].wait_recv()
+        piece = tall.at[down[d], mine]
+        send_y[d] = remote(piece, piece, ty_snd.at[d], ty_rcv.at[d], twin)
+        send_y[d].start()
+
+    for k in (2, 3, 1):
+        send_c[k].wait_recv()
+        send_f[0, k].wait_recv()
+    tokens = tok.shape[1]
+    vocab_ids = z * block + lax.broadcasted_iota(jnp.int32, (block, tokens), 0)
+    one_hot = (jnp.broadcast_to(tok[...], (block, tokens)) == vocab_ids).astype(jnp.float32)
+    one_hot = one_hot.astype(jnp.bfloat16)
+    grads = gall[z].reshape(tokens, block)
+
+    @pl.loop(0, cols // TILE)
+    def _(j):
+        at = pl.ds(pl.multiple_of(j * TILE, 128), TILE)
+        head = lax.dot_general(
+            grads, hcols[:, :, at].reshape(tokens, TILE), (((0,), (0,)), ((), ())),
+            preferred_element_type=jnp.float32,
+        )
+        embed = jnp.dot(
+            one_hot, gcols[:, :, at].reshape(tokens, TILE), preferred_element_type=jnp.float32
+        )
+        tab_out[:, at] = (head + math.sqrt(D) * embed).astype(jnp.bfloat16)
+
+    for d in (1, 3, 2):
+        send_y[d].wait_recv()
+        for k in (2, 3, 1):
+            send_f[d, k].wait_recv()
+
+    @pl.loop(0, cols // TILE)
+    def _(j):
+        at = pl.ds(pl.multiple_of(j * TILE, 128), TILE)
+        total = jnp.zeros((tokens, TILE), jnp.float32)
+        for row in range(4):
+            total = total + jnp.dot(
+                gall[row].reshape(tokens, block), tall[row, :, at], preferred_element_type=jnp.float32
+            )
+        hid_out[:, at] = total.astype(jnp.bfloat16)
+
+    for group in (send_h, send_t, send_p, send_c, send_s, send_g, send_f, send_y):
+        for copy in group.values():
+            copy.wait_send()
+
+
+def shards(hidden, cotangent, table, token_ids, target_ids, row_counts):
+    block, cols = table.shape
+    rows = hidden.shape[0]
+    tokens = token_ids.shape[0]
+    vmem = pl.BlockSpec(memory_space=pltpu.VMEM)
+    hbm = pl.BlockSpec(memory_space=pl.ANY)
+    dma = pltpu.SemaphoreType.DMA
+    return pl.pallas_call(
+        kernel,
+        out_shape=(
+            jax.ShapeDtypeStruct((tokens, cols), jnp.bfloat16),
+            jax.ShapeDtypeStruct((block, cols), jnp.bfloat16),
+        ),
+        in_specs=[hbm, hbm, hbm, vmem, vmem, pl.BlockSpec(memory_space=pltpu.SMEM)],
+        out_specs=(vmem, vmem),
+        scratch_shapes=[
+            pltpu.VMEM((4, block, cols), jnp.bfloat16),
+            pltpu.VMEM((4, rows, cols), jnp.bfloat16),
+            pltpu.VMEM((4, rows, cols), jnp.bfloat16),
+            pltpu.VMEM((4, rows, block), jnp.float32),
+            pltpu.VMEM((4, rows, block), jnp.float32),
+            pltpu.VMEM((4, 8, 128), jnp.float32),
+            pltpu.VMEM((4, 4, rows, block), jnp.bfloat16),
+            pltpu.VMEM((tokens, 128), jnp.float32),
+            dma((3,)),
+            *[dma((4,))] * 14,
+            dma((4, 4)),
+            dma((4, 4)),
+        ],
+        compiler_params=pltpu.CompilerParams(
+            collective_id=0, has_side_effects=True, vmem_limit_bytes=40 * 1024 * 1024
+        ),
+        cost_estimate=pl.CostEstimate(flops=1200000000, bytes_accessed=6000000, transcendentals=40000),
+    )(hidden, cotangent, table, token_ids[None, :], target_ids[None, :], row_counts)
+
+
 def solution(mesh):
+    sizes = tuple(mesh.shape[axis] for axis in ("groups", "vocab", "dp", "rep"))
+
+    def part(hidden, cotangent, table, token_ids, target_ids, row_counts):
+        block, cols = table.shape
+        fits = (
+            sizes == (2, 4, 2, 2)
+            and hidden.shape[0] == ROW_LEN
+            and cols % TILE == 0
+            and block == 256
+            and token_ids.shape[0] == 256
+        )
+        run = shards if fits else plain
+        return run(hidden, cotangent, table, token_ids, target_ids, row_counts)
+
     in_specs = (
         P(("groups", "dp", "rep"), None),
         P(("groups", "dp", "rep"), None),
@@ -69,4 +290,4 @@
         P("groups"),
     )
     out_specs = (P("groups", ("dp", "rep")), P(("groups", "vocab"), ("dp", "rep")))
-    return jax.shard_map(shards, mesh=mesh, in_specs=in_specs, out_specs=out_specs, check_vma=False)
+    return jax.shard_map(part, mesh=mesh, in_specs=in_specs, out_specs=out_specs, check_vma=False)

time: 148 us -> 64.8 us (0.44)
  blocking collectives: 84.6 us -> 0 us
  Pallas kernels: 0 us -> 58.4 us
  waiting for transfers between devices: 33.2 us -> 0 us
  between operations: 14.1 us -> 0.67 us
  starting transfers between devices: 7.99 us -> 0 us
  matrix products: 3.06 us -> 0 us
  local copies, waits for them, and re-layouts: 2.99 us -> 5.5 us
  other arithmetic: 1.89 us -> 0 us
    psum x2 -> x0, blocking collectives: 79.2 us -> none  [the longest x1 47 us: shards(): hidden_grad = lax.psum(partial_sum, 'vocab').astype(jnp.bfloat16)]
    pallas_call x0 -> x1, Pallas kernels: none -> 58.4 us  [shards(): pl.pallas_call(kernel, out_shape=(jax.ShapeDtypeStruct((tokens, cols), jn...]
    all_to_all x2 -> x0, waiting for transfers between devices: 16.9 us -> none  [the longest x1 8.67 us: shards(): lax.all_to_all(hidden, ('dp', 'rep'), split_axis=1, concat_axis=0, tiled=...]
    reduce_scatter x1 -> x0, waiting for transfers between devices: 16.4 us -> none  [shards(): lax.psum_scatter(lax.dot_general(table, h_cols, (((1,), (1,)), ((), ())),...]
    all_to_all x2 -> x0, starting transfers between devices: 7.95 us -> none  [the longest x1 4.34 us: shards(): lax.all_to_all(hidden, ('dp', 'rep'), split_axis=1, concat_axis=0, tiled=...]
    unnamed x10 -> x14, local copies, waits for them, and re-layouts: 0.02 us -> 5.5 us
    all_gather x1 -> x0, blocking collectives: 5.43 us -> none  [shards(): grads = lax.all_gather(grad, ('dp', 'rep'), axis=0, tiled=True)]
    dot_general x4 -> x0, matrix products: 3.06 us -> none  [the longest x1 1.16 us: shards(): head = jnp.dot(grads, h_cols, preferred_element_type=jnp.float32)]
  transfers between devices with their start and end apart: 3 -> 0, of which waited for: 3 -> 0; matrix products, arithmetic and copies ran while one was open for 2% -> 0% of each run, Pallas kernels for 0% -> 0%
where the time goes in v1:
time: 64.8 us; the launch traced here: 64.5 us
  Pallas kernels  58.4 us (90%)
  local copies, waits for them, and re-layouts  5.5 us (8%)
  between operations  0.67 us (1%)
    pallas_call x1, Pallas kernels, shards(): pl.pallas_call(kernel, out_shape=(jax.ShapeDtypeStruct((tokens, cols), jn...  58.4 us
    unnamed x14, local copies, waits for them, and re-layouts  5.5 us

profile of v1, /device:TPU:0, one launch (start us, length us, event | category | flops | bytes accessed | tf_op | source)
XLA Modules:
  0.0 64.5 jit_solution(1359101063916319044)
XLA Ops:
  0.6 0.0 copy-start.4
  0.6 0.0 copy-start.3
  0.7 0.0 copy-start.5
  0.7 0.7 %copy-done.4 = s32[256]{0:T(256)S(1)} copy-done((s32[256]{0:T(256)S(1)}, s32[256]{0:T(256)}, u32[]{:S(2)}) %copy-start.4) | copy-done | bytes 1048
  1.3 0.0 copy-done.3
  1.3 0.0 copy-done.5
  1.3 0.0 copy-start
  1.3 1.1 %copy-done = bf16[64,4608]{1,0:T(8,128)(2,1)S(1)} copy-done((bf16[64,4608]{1,0:T(8,128)(2,1)S(1)}, bf16[64,4608]{1,0:T(8,128)(2,1)}, u32[]{:S(2)}) %copy-start) | copy-done | bytes 589848
  2.4 0.0 copy-start.1
  2.4 1.1 %copy-done.1 = bf16[64,4608]{1,0:T(8,128)(2,1)S(1)} copy-done((bf16[64,4608]{1,0:T(8,128)(2,1)S(1)}, bf16[64,4608]{1,0:T(8,128)(2,1)}, u32[]{:S(2)}) %copy-start.1) | copy-done | bytes 589848
  3.5 0.0 copy-start.2
  3.5 1.1 %copy-done.2 = bf16[256,1152]{1,0:T(8,128)(2,1)S(1)} copy-done((bf16[256,1152]{1,0:T(8,128)(2,1)S(1)}, bf16[256,1152]{1,0:T(8,128)(2,1)}, u32[]{:S(2)}) %copy-start.2) | copy-done | bytes 589848
  4.5 58.4 %shard_map.77 = (bf16[256,1152]{1,0:T(8,128)(2,1)S(1)}, bf16[256,1152]{1,0:T(8,128)(2,1)S(1)}) custom-call(bf16[64,4608]{1,0:T(8,128)(2,1)S(1)} %copy-done, bf16[64,4608]{1,0:T(8,128)(2,1)S(1)} %copy-done.1, bf16[256,1152]{1,0:T(8,128)(2,1)S(1)} %copy-done.2, s32[1,256]{1,0:T(1,128)S(1)} %bitcast.2, s32[1,256]{1,0:T(1,128)S(1)} %bitcast.3, s32[4]{0:T(128)S(1)} %copy-done.5), custom_call_target="tpu_custom_call" | custom-call | flops 1200000000 | bytes 6000000 | tf_op jit(solution)/shard_map/pallas_call | solution.py:240
  62.9 0.8 %copy.10 = bf16[256,1152]{1,0:T(8,128)(2,1)} copy(bf16[256,1152]{1,0:T(8,128)(2,1)S(1)} %get-tuple-element.4) | data formatting | bytes 1179648
  63.7 0.8 %copy.11 = bf16[256,1152]{1,0:T(8,128)(2,1)} copy(bf16[256,1152]{1,0:T(8,128)(2,1)S(1)} %get-tuple-element.5) | data formatting | bytes 1179648
Async XLA Ops:
  0.6 0.7 %copy-start.4 = (s32[256]{0:T(256)S(1)}, s32[256]{0:T(256)}, u32[]{:S(2)}) copy-start(s32[256]{0:T(256)} %param.10) | copy-start | bytes 3076
  0.6 0.7 %copy-start.3 = (s32[256]{0:T(256)S(1)}, s32[256]{0:T(256)}, u32[]{:S(2)}) copy-start(s32[256]{0:T(256)} %param.9) | copy-start | bytes 3076
  0.7 0.7 %copy-start.5 = (s32[4]{0:T(128)S(1)}, s32[4]{0:T(128)}, u32[]{:S(2)}) copy-start(s32[4]{0:T(128)} %cnt.1) | copy-start | bytes 52
  1.3 1.1 %copy-start = (bf16[64,4608]{1,0:T(8,128)(2,1)S(1)}, bf16[64,4608]{1,0:T(8,128)(2,1)}, u32[]{:S(2)}) copy-start(bf16[64,4608]{1,0:T(8,128)(2,1)} %hid.1) | copy-start | bytes 1769476
  2.4 1.1 %copy-start.1 = (bf16[64,4608]{1,0:T(8,128)(2,1)S(1)}, bf16[64,4608]{1,0:T(8,128)(2,1)}, u32[]{:S(2)}) copy-start(bf16[64,4608]{1,0:T(8,128)(2,1)} %cot.1) | copy-start | bytes 1769476
  3.5 1.1 %copy-start.2 = (bf16[256,1152]{1,0:T(8,128)(2,1)S(1)}, bf16[256,1152]{1,0:T(8,128)(2,1)}, u32[]{:S(2)}) copy-start(bf16[256,1152]{1,0:T(8,128)(2,1)} %tab.1) | copy-start | bytes 1769476

commit v2 on v1

--- a/solution.py
+++ b/solution.py
@@ -113,12 +113,46 @@
     for copy in send_h.values():
         copy.start()
     mine = pl.ds(pl.multiple_of(half * y, half), half)
-    send_t = {
-        d: remote(tab.at[mine], tall.at[z, mine], tz_snd.at[d], tz_rcv.at[d], up_id[d])
-        for d in (1, 3, 2)
-    }
-    for copy in send_t.values():
-        copy.start()
+
+    def relay(s, way):
+        row = z - way * (s - 1)
+        src = tab.at[mine] if s == 1 else tall.at[row, mine]
+        lane = s if way == 1 else s + 4
+        copy = remote(src, tall.at[row, mine], tz_snd.at[lane], tz_rcv.at[lane], {"vocab": z + way})
+        on = (z < 3) & (row >= 0) if way == 1 else (z > 0) & (row <= 3)
+        return on, copy
+
+    def landed(s, way):
+        row = z - way * s
+        piece = tall.at[row, mine]
+        lane = s if way == 1 else s + 4
+        came = remote(piece, piece, tz_snd.at[lane], tz_rcv.at[lane], {"vocab": z + way})
+        over = remote(piece, piece, ty_snd.at[lane], ty_rcv.at[lane], twin)
+        on = row >= 0 if way == 1 else row <= 3
+        return on, came, over
+
+    def pass_on(s):
+        for way in (1, -1):
+            on, came, over = landed(s, way)
+
+            @pl.when(on)
+            def _():
+                came.wait_recv()
+                over.start()
+
+            if s < 3:
+                on, copy = relay(s + 1, way)
+
+                @pl.when(on)
+                def _():
+                    copy.start()
+
+    for way in (1, -1):
+        on, copy = relay(1, way)
+
+        @pl.when(on)
+        def _():
+            copy.start()
 
     ids = jnp.broadcast_to(tgt[...].astype(jnp.float32), (128, tgt.shape[1]))
     tcol[...] = ids.T
@@ -141,6 +175,7 @@
     }
     for copy in send_c.values():
         copy.start()
+    pass_on(1)
 
     raw = part[0]
     for k in (1, 2, 3):
@@ -173,24 +208,27 @@
         copy.start()
     send_f = {}
 
-    def hand_on(d, row):
-        for k in (2, 3, 1):
-            piece = gall.at[row, p]
-            send_f[d, k] = remote(piece, piece, f_snd.at[d, k], f_rcv.at[d, k], near_id[k])
-            send_f[d, k].start()
-
-    hand_on(0, z)
-    send_y = {}
+    def hand_on(d, row, k):
+        piece = gall.at[row, place[2] if k == 3 else p]
+        to = near_id[1 if k == 3 else k]
+        send_f[d, k] = remote(piece, piece, f_snd.at[d, k], f_rcv.at[d, k], to)
+        send_f[d, k].start()
+
+    hand_on(0, z, 2)
+    hand_on(0, z, 1)
+    pass_on(2)
     for d in (1, 3, 2):
         send_g[d].wait_recv()
-        hand_on(d, down[d])
-        send_t[d].wait_recv()
-        piece = tall.at[down[d], mine]
-        send_y[d] = remote(piece, piece, ty_snd.at[d], ty_rcv.at[d], twin)
-        send_y[d].start()
+        hand_on(d, down[d], 2)
+        hand_on(d, down[d], 1)
+    for d in (0, 1, 3, 2):
+        send_f[d, 2].wait_recv()
+        hand_on(d, down[d] if d else z, 3)
+    pass_on(3)
 
     for k in (2, 3, 1):
         send_c[k].wait_recv()
+    for k in (1, 3):
         send_f[0, k].wait_recv()
     tokens = tok.shape[1]
     vocab_ids = z * block + lax.broadcasted_iota(jnp.int32, (block, tokens), 0)
@@ -211,9 +249,21 @@
         tab_out[:, at] = (head + math.sqrt(D) * embed).astype(jnp.bfloat16)
 
     for d in (1, 3, 2):
-        send_y[d].wait_recv()
-        for k in (2, 3, 1):
+        for k in (1, 3):
             send_f[d, k].wait_recv()
+    for s in (1, 2, 3):
+        for way in (1, -1):
+            on, _, over = landed(s, way)
+
+            @pl.when(on)
+            def _():
+                over.wait()
+
+            on, copy = relay(s, way)
+
+            @pl.when(on)
+            def _():
+                copy.wait_send()
 
     @pl.loop(0, cols // TILE)
     def _(j):
@@ -225,7 +275,7 @@
             )
         hid_out[:, at] = total.astype(jnp.bfloat16)
 
-    for group in (send_h, send_t, send_p, send_c, send_s, send_g, send_f, send_y):
+    for group in (send_h, send_p, send_c, send_s, send_g, send_f):
         for copy in group.values():
             copy.wait_send()
 
@@ -255,12 +305,14 @@
             pltpu.VMEM((4, 4, rows, block), jnp.bfloat16),
             pltpu.VMEM((tokens, 128), jnp.float32),
             dma((3,)),
-            *[dma((4,))] * 14,
+            *[dma((4,))] * 4,
+            *[dma((8,))] * 4,
+            *[dma((4,))] * 6,
             dma((4, 4)),
             dma((4, 4)),
         ],
         compiler_params=pltpu.CompilerParams(
-            collective_id=0, has_side_effects=True, vmem_limit_bytes=40 * 1024 * 1024
+            collective_id=0, has_side_effects=True, vmem_limit_bytes=60 * 1024 * 1024
         ),
         cost_estimate=pl.CostEstimate(flops=1200000000, bytes_accessed=6000000, transcendentals=40000),
     )(hidden, cotangent, table, token_ids[None, :], target_ids[None, :], row_counts)

time: 64.8 us -> 48.8 us (0.75)
  Pallas kernels: 58.4 us -> 45.2 us
  local copies, waits for them, and re-layouts: 5.5 us -> 2.8 us
    pallas_call x1, Pallas kernels: 58.4 us -> 45.2 us  [shards(): pl.pallas_call(kernel, out_shape=(jax.ShapeDtypeStruct((tokens, cols), jn...]
    unnamed x14 -> x4, local copies, waits for them, and re-layouts: 5.5 us -> 2.8 us
where the time goes in v2:
time: 48.8 us; the launch traced here: 48.7 us
  Pallas kernels  45.2 us (93%)
  local copies, waits for them, and re-layouts  2.8 us (6%)
  between operations  0.65 us (1%)
    pallas_call x1, Pallas kernels, shards(): pl.pallas_call(kernel, out_shape=(jax.ShapeDtypeStruct((tokens, cols), jn...  45.2 us
    unnamed x4, local copies, waits for them, and re-layouts  2.8 us

profile of v2, /device:TPU:0, one launch (start us, length us, event | category | flops | bytes accessed | tf_op | source)
XLA Modules:
  0.0 48.7 jit_solution(8812667597294217124)
XLA Ops:
  0.6 45.2 %shard_map.77 = (bf16[256,1152]{1,0:T(8,128)(2,1)}, bf16[256,1152]{1,0:T(8,128)(2,1)}) custom-call(bf16[64,4608]{1,0:T(8,128)(2,1)} %hid.1, bf16[64,4608]{1,0:T(8,128)(2,1)} %cot.1, bf16[256,1152]{1,0:T(8,128)(2,1)} %tab.1, s32[1,256]{1,0:T(1,128)} %bitcast.2, s32[1,256]{1,0:T(1,128)} %bitcast.3, s32[4]{0:T(128)} %cnt.1), custom_call_target="tpu_custom_call" | custom-call | flops 1200000000 | bytes 6000000 | tf_op jit(solution)/shard_map/pallas_call | solution.py:290
  45.9 0.0 copy-start
  45.9 2.0 %copy.10 = bf16[256,1152]{1,0:T(8,128)(2,1)} copy(bf16[256,1152]{1,0:T(8,128)(2,1)} %get-tuple-element.4) | data formatting | bytes 1179648
  47.8 0.0 copy-done
  47.9 0.8 %copy.11 = bf16[256,1152]{1,0:T(8,128)(2,1)} copy(bf16[256,1152]{1,0:T(8,128)(2,1)S(1)} %copy-done) | data formatting | bytes 1179648
Async XLA Ops:
  45.9 2.0 %copy-start = (bf16[256,1152]{1,0:T(8,128)(2,1)S(1)}, bf16[256,1152]{1,0:T(8,128)(2,1)}, u32[]{:S(2)}) copy-start(bf16[256,1152]{1,0:T(8,128)(2,1)} %get-tuple-element.5) | copy-start | bytes 1769476

commit v3 on v2

--- a/solution.py
+++ b/solution.py
@@ -112,28 +112,30 @@
     }
     for copy in send_h.values():
         copy.start()
-    mine = pl.ds(pl.multiple_of(half * y, half), half)
-
-    def relay(s, way):
+
+    def strip(part):
+        return pl.ds(pl.multiple_of(half * y + half // 2 * part, half // 2), half // 2)
+
+    def relay(s, way, part):
         row = z - way * (s - 1)
-        src = tab.at[mine] if s == 1 else tall.at[row, mine]
-        lane = s if way == 1 else s + 4
-        copy = remote(src, tall.at[row, mine], tz_snd.at[lane], tz_rcv.at[lane], {"vocab": z + way})
+        src = tab.at[strip(part)] if s == 1 else tall.at[row, strip(part)]
+        lane = (s if way == 1 else s + 4) + 8 * part
+        copy = remote(src, tall.at[row, strip(part)], tz_snd.at[lane], tz_rcv.at[lane], {"vocab": z + way})
         on = (z < 3) & (row >= 0) if way == 1 else (z > 0) & (row <= 3)
         return on, copy
 
-    def landed(s, way):
+    def landed(s, way, part):
         row = z - way * s
-        piece = tall.at[row, mine]
-        lane = s if way == 1 else s + 4
+        piece = tall.at[row, strip(part)]
+        lane = (s if way == 1 else s + 4) + 8 * part
         came = remote(piece, piece, tz_snd.at[lane], tz_rcv.at[lane], {"vocab": z + way})
         over = remote(piece, piece, ty_snd.at[lane], ty_rcv.at[lane], twin)
         on = row >= 0 if way == 1 else row <= 3
         return on, came, over
 
-    def pass_on(s):
+    def pass_on(s, part):
         for way in (1, -1):
-            on, came, over = landed(s, way)
+            on, came, over = landed(s, way, part)
 
             @pl.when(on)
             def _():
@@ -141,18 +143,19 @@
                 over.start()
 
             if s < 3:
-                on, copy = relay(s + 1, way)
+                on, copy = relay(s + 1, way, part)
 
                 @pl.when(on)
                 def _():
                     copy.start()
 
-    for way in (1, -1):
-        on, copy = relay(1, way)
-
-        @pl.when(on)
-        def _():
-            copy.start()
+    for part_of in (0, 1):
+        for way in (1, -1):
+            on, copy = relay(1, way, part_of)
+
+            @pl.when(on)
+            def _():
+                copy.start()
 
     ids = jnp.broadcast_to(tgt[...].astype(jnp.float32), (128, tgt.shape[1]))
     tcol[...] = ids.T
@@ -161,6 +164,8 @@
         copy.wait()
     send_p = {}
     for k in (0, 1, 2, 3):
+        if k == 2:
+            pass_on(1, 0)
         if k:
             send_h[k].wait_recv()
         part[k] = lax.dot_general(
@@ -175,7 +180,7 @@
     }
     for copy in send_c.values():
         copy.start()
-    pass_on(1)
+    pass_on(1, 1)
 
     raw = part[0]
     for k in (1, 2, 3):
@@ -216,15 +221,17 @@
 
     hand_on(0, z, 2)
     hand_on(0, z, 1)
-    pass_on(2)
+    pass_on(2, 0)
     for d in (1, 3, 2):
         send_g[d].wait_recv()
         hand_on(d, down[d], 2)
         hand_on(d, down[d], 1)
+    pass_on(2, 1)
     for d in (0, 1, 3, 2):
         send_f[d, 2].wait_recv()
         hand_on(d, down[d] if d else z, 3)
-    pass_on(3)
+    pass_on(3, 0)
+    pass_on(3, 1)
 
     for k in (2, 3, 1):
         send_c[k].wait_recv()
@@ -251,15 +258,15 @@
     for d in (1, 3, 2):
         for k in (1, 3):
             send_f[d, k].wait_recv()
-    for s in (1, 2, 3):
+    for s, part_of in [(s, part_of) for s in (1, 2, 3) for part_of in (0, 1)]:
         for way in (1, -1):
-            on, _, over = landed(s, way)
+            on, _, over = landed(s, way, part_of)
 
             @pl.when(on)
             def _():
                 over.wait()
 
-            on, copy = relay(s, way)
+            on, copy = relay(s, way, part_of)
 
             @pl.when(on)
             def _():
@@ -306,7 +313,7 @@
             pltpu.VMEM((tokens, 128), jnp.float32),
             dma((3,)),
             *[dma((4,))] * 4,
-            *[dma((8,))] * 4,
+            *[dma((16,))] * 4,
             *[dma((4,))] * 6,
             dma((4, 4)),
             dma((4, 4)),

time: 48.8 us -> 43.9 us (0.90)
  Pallas kernels: 45.2 us -> 40.3 us
    pallas_call x1, Pallas kernels: 45.2 us -> 40.3 us  [shards(): pl.pallas_call(kernel, out_shape=(jax.ShapeDtypeStruct((tokens, cols), jn...]
where the time goes in v3:
time: 43.9 us; the launch traced here: 43.8 us
  Pallas kernels  40.3 us (92%)
  local copies, waits for them, and re-layouts  2.8 us (6%)
  between operations  0.65 us (1%)
    pallas_call x1, Pallas kernels, shards(): pl.pallas_call(kernel, out_shape=(jax.ShapeDtypeStruct((tokens, cols), jn...  40.3 us
    unnamed x4, local copies, waits for them, and re-layouts  2.8 us

profile of v3, /device:TPU:0, one launch (start us, length us, event | category | flops | bytes accessed | tf_op | source)
XLA Modules:
  0.0 43.8 jit_solution(3854041215435342023)
XLA Ops:
  0.6 40.3 %shard_map.77 = (bf16[256,1152]{1,0:T(8,128)(2,1)}, bf16[256,1152]{1,0:T(8,128)(2,1)}) custom-call(bf16[64,4608]{1,0:T(8,128)(2,1)} %hid.1, bf16[64,4608]{1,0:T(8,128)(2,1)} %cot.1, bf16[256,1152]{1,0:T(8,128)(2,1)} %tab.1, s32[1,256]{1,0:T(1,128)} %bitcast.2, s32[1,256]{1,0:T(1,128)} %bitcast.3, s32[4]{0:T(128)} %cnt.1), custom_call_target="tpu_custom_call" | custom-call | flops 1200000000 | bytes 6000000 | tf_op jit(solution)/shard_map/pallas_call | solution.py:297
  41.0 0.0 copy-start
  41.0 2.0 %copy.10 = bf16[256,1152]{1,0:T(8,128)(2,1)} copy(bf16[256,1152]{1,0:T(8,128)(2,1)} %get-tuple-element.4) | data formatting | bytes 1179648
  42.9 0.0 copy-done
  43.0 0.8 %copy.11 = bf16[256,1152]{1,0:T(8,128)(2,1)} copy(bf16[256,1152]{1,0:T(8,128)(2,1)S(1)} %copy-done) | data formatting | bytes 1179648
Async XLA Ops:
  41.0 2.0 %copy-start = (bf16[256,1152]{1,0:T(8,128)(2,1)S(1)}, bf16[256,1152]{1,0:T(8,128)(2,1)}, u32[]{:S(2)}) copy-start(bf16[256,1152]{1,0:T(8,128)(2,1)} %get-tuple-element.5) | copy-start | bytes 1769476

commit v4 on v3

--- a/solution.py
+++ b/solution.py
@@ -230,7 +230,8 @@
     for d in (0, 1, 3, 2):
         send_f[d, 2].wait_recv()
         hand_on(d, down[d] if d else z, 3)
-    pass_on(3, 0)
+        if d == 1:
+            pass_on(3, 0)
     pass_on(3, 1)
 
     for k in (2, 3, 1):
@@ -287,6 +288,11 @@
             copy.wait_send()
 
 
+def hand_out(hid, tab, hid_out, tab_out):
+    hid_out[...] = hid[...]
+    tab_out[...] = tab[...]
+
+
 def shards(hidden, cotangent, table, token_ids, target_ids, row_counts):
     block, cols = table.shape
     rows = hidden.shape[0]
@@ -294,7 +300,7 @@
     vmem = pl.BlockSpec(memory_space=pltpu.VMEM)
     hbm = pl.BlockSpec(memory_space=pl.ANY)
     dma = pltpu.SemaphoreType.DMA
-    return pl.pallas_call(
+    results = pl.pallas_call(
         kernel,
         out_shape=(
             jax.ShapeDtypeStruct((tokens, cols), jnp.bfloat16),
@@ -323,6 +329,13 @@
         ),
         cost_estimate=pl.CostEstimate(flops=1200000000, bytes_accessed=6000000, transcendentals=40000),
     )(hidden, cotangent, table, token_ids[None, :], target_ids[None, :], row_counts)
+    return pl.pallas_call(
+        hand_out,
+        out_shape=tuple(jax.ShapeDtypeStruct(a.shape, a.dtype) for a in results),
+        grid=(2,),
+        in_specs=[pl.BlockSpec((a.shape[0] // 2, cols), lambda i: (i, 0)) for a in results],
+        out_specs=tuple(pl.BlockSpec((a.shape[0] // 2, cols), lambda i: (i, 0)) for a in results),
+    )(*results)
 
 
 def solution(mesh):

time: 43.9 us -> 42.9 us (0.977)
  local copies, waits for them, and re-layouts: 2.8 us -> 0 us
  Pallas kernels: 40.3 us -> 42.1 us
    unnamed x4 -> x0, local copies, waits for them, and re-layouts: 2.8 us -> none
    pallas_call x0 -> x1, Pallas kernels: none -> 2.11 us  [shards(): pl.pallas_call(hand_out, out_shape=tuple((jax.ShapeDtypeStruct(a.shape, a...]
where the time goes in v4:
time: 42.9 us; the launch traced here: 42.7 us
  Pallas kernels  42.1 us (98%)
  between operations  0.64 us (1%)
    pallas_call x1, Pallas kernels, shards(): pl.pallas_call(kernel, out_shape=(jax.ShapeDtypeStruct((tokens, cols), jn...  40 us
    pallas_call x1, Pallas kernels, shards(): pl.pallas_call(hand_out, out_shape=tuple((jax.ShapeDtypeStruct(a.shape, a...  2.11 us

profile of v4, /device:TPU:0, one launch (start us, length us, event | category | flops | bytes accessed | tf_op | source)
XLA Modules:
  0.0 42.7 jit_solution(10675419866696890240)
XLA Ops:
  0.6 40.0 %shard_map.77 = (bf16[256,1152]{1,0:T(8,128)(2,1)}, bf16[256,1152]{1,0:T(8,128)(2,1)}) custom-call(bf16[64,4608]{1,0:T(8,128)(2,1)} %hid.1, bf16[64,4608]{1,0:T(8,128)(2,1)} %cot.1, bf16[256,1152]{1,0:T(8,128)(2,1)} %tab.1, s32[1,256]{1,0:T(1,128)} %bitcast.2, s32[1,256]{1,0:T(1,128)} %bitcast.3, s32[4]{0:T(128)} %cnt.1), custom_call_target="tpu_custom_call" | custom-call | flops 1200000000 | bytes 6000000 | tf_op jit(solution)/shard_map/pallas_call | solution.py:303
  40.6 2.1 %shard_map.78 = (bf16[256,1152]{1,0:T(8,128)(2,1)}, bf16[256,1152]{1,0:T(8,128)(2,1)}) custom-call(bf16[256,1152]{1,0:T(8,128)(2,1)} %get-tuple-element.4.hid, bf16[256,1152]{1,0:T(8,128)(2,1)} %get-tuple-element.5.tab), custom_call_target="tpu_custom_call" | custom-call | tf_op jit(solution)/shard_map/pallas_call | solution.py:332

commit v5 on v4

--- a/solution.py
+++ b/solution.py
@@ -201,6 +201,7 @@
     slot = lax.broadcasted_iota(jnp.int32, (ROW_LEN, block), 0)
     weight = jnp.where(slot < count, ROW_LEN / count.astype(jnp.float32), 0.0)
     slope = 1.0 - squash * squash
+    pass_on(2, 0)
     for copy in send_s.values():
         copy.wait_recv()
     whole = tot[0] + tot[1] + tot[2] + tot[3]
@@ -221,7 +222,6 @@
 
     hand_on(0, z, 2)
     hand_on(0, z, 1)
-    pass_on(2, 0)
     for d in (1, 3, 2):
         send_g[d].wait_recv()
         hand_on(d, down[d], 2)

time: 42.9 us -> 42.5 us (level)
  no operation moved by 1% of the time
where the time goes in v5:
time: 42.5 us; the launch traced here: 42.4 us
  Pallas kernels  41.7 us (98%)
  between operations  0.64 us (2%)
    pallas_call x1, Pallas kernels, shards(): pl.pallas_call(kernel, out_shape=(jax.ShapeDtypeStruct((tokens, cols), jn...  39.6 us
    pallas_call x1, Pallas kernels, shards(): pl.pallas_call(hand_out, out_shape=tuple((jax.ShapeDtypeStruct(a.shape, a...  2.11 us

profile of v5, /device:TPU:0, one launch (start us, length us, event | category | flops | bytes accessed | tf_op | source)
XLA Modules:
  0.0 42.4 jit_solution(379736006360531942)
XLA Ops:
  0.6 39.6 %shard_map.77 = (bf16[256,1152]{1,0:T(8,128)(2,1)}, bf16[256,1152]{1,0:T(8,128)(2,1)}) custom-call(bf16[64,4608]{1,0:T(8,128)(2,1)} %hid.1, bf16[64,4608]{1,0:T(8,128)(2,1)} %cot.1, bf16[256,1152]{1,0:T(8,128)(2,1)} %tab.1, s32[1,256]{1,0:T(1,128)} %bitcast.2, s32[1,256]{1,0:T(1,128)} %bitcast.3, s32[4]{0:T(128)} %cnt.1), custom_call_target="tpu_custom_call" | custom-call | flops 1200000000 | bytes 6000000 | tf_op jit(solution)/shard_map/pallas_call | solution.py:303
  40.3 2.1 %shard_map.78 = (bf16[256,1152]{1,0:T(8,128)(2,1)}, bf16[256,1152]{1,0:T(8,128)(2,1)}) custom-call(bf16[256,1152]{1,0:T(8,128)(2,1)} %get-tuple-element.4.hid, bf16[256,1152]{1,0:T(8,128)(2,1)} %get-tuple-element.5.tab), custom_call_target="tpu_custom_call" | custom-call | tf_op jit(solution)/shard_map/pallas_call | solution.py:332
